TPU v7x, 128 devices: a whole 4x4x4 slice. The times are simulated.
128 devices in a mesh: gx: 8 (over z_lo, y), gy: 16 (over x, z_hi, core).
Axes of the slice: x: 4, y: 4, z: 4 (z_hi: 2, z_lo: 2; z = z_hi * 2 + z_lo), core: 2. Of those that a mesh axis runs over, the one named last changes fastest.
Arguments:
- levels: int32 [8, 128, 16384], P(None, 'gx', 'gy'), may hold values from 0 to 7
- probe_bits: int32 [8, 8, 128, 16384], P(None, None, 'gx', 'gy'), may hold values from 0 to 1
Outputs:
- green: float32 [2, 8192, 64], P(None, ('gx', 'gy'))
- last_vector: float32 [8, 8, 128, 16384], P(None, None, 'gx', 'gy')
All inputs are finite; a program needn't handle non-finite values.
Results may differ from a plain program's by a relative error of at most 0.00011.
Values sent between devices are 32-bit elements; how exact they have to be, the bound alone decides.
A program may use at most 128 MiB of HBM per device.

v0:
```python
import functools
import math

import jax
import jax.numpy as jnp
from jax import lax
from jax.sharding import Mesh
from jax.sharding import PartitionSpec as P

STEPS = 4
LEVELS = 8
NE = 8192
GX_GY = ("gx_0", "gx_1", "gy_0", "gy_1", "gy_2")
GX = ("gx_0", "gx_1")
GY = ("gy_0", "gy_1", "gy_2")


disorder_width = 4.0
field_strength = 3.0
spectral_scale = 10.0
energy_edge = 0.9


def one_axis_at_a_time(array, axes):
    return functools.reduce(lax.psum, axes, array)


def extended(array, sides, width):
    edges = {}
    for axis, dim in sides:
        peers, length = (lax.axis_size(axis), array.shape[dim])
        up = [(i, (i + 1) % peers) for i in range(peers)]
        last = lax.slice_in_dim(array, length - width, length, axis=dim)
        first = lax.slice_in_dim(array, 0, width, axis=dim)
        edges[dim] = (
            lax.ppermute(last, axis, up),
            lax.ppermute(first, axis, [(b, a) for a, b in up]),
        )
    done = []
    for _, dim in sides:
        low, high = edges[dim]
        around = [(width, width) if d in done else (0, 0) for d in range(array.ndim)]
        array = jnp.concatenate([jnp.pad(low, around), array, jnp.pad(high, around)], axis=dim)
        done.append(dim)
    return array


def jackson_weights(count):
    total = count + 1.0
    values = []
    for order in range(count):
        damping = (
            (count - order + 1.0) * math.cos(math.pi * order / total)
            + math.sin(math.pi * order / total) / math.tan(math.pi / total)
        ) / total
        values.append(damping if order == 0 else 2.0 * damping)
    return jnp.asarray(values, dtype=jnp.float32)


def energy_tables(energy_index, count, total_energies):
    phase = math.pi * (energy_index.astype(jnp.float32) + 0.5) / total_energies
    theta = jnp.arccos(energy_edge * jnp.cos(phase))
    orders = jnp.arange(count).astype(jnp.float32)
    weights = jackson_weights(count)
    angles = theta[:, None] * orders[None, :]
    denominator = jnp.sin(theta)[:, None]
    real_part = -weights[None, :] * jnp.sin(angles) / denominator
    imag_part = -weights[None, :] * jnp.cos(angles) / denominator
    return (real_part, imag_part)


def hopping(padded, onsite):
    center = padded[:, :, 1:-1, 1:-1]
    beside = padded[:, :, 2:, 1:-1] + padded[:, :, :-2, 1:-1]
    beside = beside + padded[:, :, 1:-1, 2:] + padded[:, :, 1:-1, :-2]
    zeros_plane = jnp.zeros_like(center[:, :1])
    beside = beside + jnp.concatenate([center[:, 1:], zeros_plane], 1)
    beside = beside + jnp.concatenate([zeros_plane, center[:, :-1]], 1)
    return (onsite[None] * center - beside) / spectral_scale


def inner_matrix(first, second):
    left = first.reshape(first.shape[0], -1)
    right = second.reshape(second.shape[0], -1)
    return jnp.dot(
        left, right.T, precision=lax.Precision.HIGHEST, preferred_element_type=jnp.float32
    )


def step_pair(vectors, step):
    local = jnp.stack(
        [inner_matrix(vectors[step], vectors[step]), inner_matrix(vectors[step], vectors[step + 1])]
    )
    return one_axis_at_a_time(local, GX_GY)


def moments_from(grams, sites):
    first = grams[0] / sites
    second = grams[1] / sites
    result = [first, second]
    for order in range(1, grams.shape[0] // 2):
        result.append(2.0 * grams[2 * order] / sites - first)
        result.append(2.0 * grams[2 * order + 1] / sites - second)
    stacked = jnp.stack(result)
    return stacked.reshape(stacked.shape[0], -1)


def on_device(levels, probe_bits):
    planes, height, breadth = levels.shape
    count_gx = lax.axis_size(GX)
    count_gy = lax.axis_size(GY)
    total_rows = height * count_gx
    sites = planes * total_rows * breadth * count_gy
    row_index = (lax.axis_index(GX) * height + jnp.arange(height)).astype(jnp.float32)
    onsite = (
        disorder_width * (levels.astype(jnp.float32) / (LEVELS - 1) - 0.5)
        + field_strength * ((row_index + 0.5) / total_rows - 0.5)[None, :, None]
    )
    vectors = [(2 * probe_bits - 1).astype(jnp.float32)]
    for step in range(STEPS):
        padded = extended(vectors[-1], ((GX, 2), (GY, 3)), 1)
        hopped = hopping(padded, onsite)
        if step == 0:
            vectors.append(hopped)
        else:
            vectors.append(2.0 * hopped - vectors[-2])
    grams = jnp.concatenate([step_pair(vectors, step) for step in range(STEPS)], 0)
    moments = moments_from(grams, sites)
    per_device = NE // (count_gx * count_gy)
    start = (lax.axis_index(GX) * count_gy + lax.axis_index(GY)) * per_device
    energy_index = start + jnp.arange(per_device)
    real_part, imag_part = energy_tables(energy_index, grams.shape[0], NE)
    green_real = jnp.dot(
        real_part, moments, precision=lax.Precision.HIGHEST, preferred_element_type=jnp.float32
    )
    green_imag = jnp.dot(
        imag_part, moments, precision=lax.Precision.HIGHEST, preferred_element_type=jnp.float32
    )
    return (jnp.stack([green_real, green_imag]), vectors[-1])


def solution(mesh):
    torus = Mesh(mesh.devices.reshape(2, 4, 4, 2, 2), ("gx_0", "gx_1", "gy_0", "gy_1", "gy_2"))
    return jax.shard_map(
        on_device,
        mesh=torus,
        in_specs=(P(None, GX, GY), P(None, None, GX, GY)),
        out_specs=(P(None, GX_GY, None), P(None, None, GX, GY)),
        check_vma=False,
    )
```

profile of v0, /device:TPU:1, one launch (start us, length us, event | category | flops | bytes accessed | tf_op | source)
XLA Modules:
  0.0 264.3 jit_solution(15500787697427943547)
XLA Ops:
  0.6 5.2 %fusion.41 = f32[8,8,16,1024]{3,1,2,0:T(8,128)S(1)} fusion(s32[8,8,16,1024]{3,2,1,0:T(8,128)} %param.4), kind=kLoop, calls=%fused_computation.76 | loop fusion | flops 3145728 | bytes 8388608 | tf_op jit(solution)/shard_map/convert_element_type | solution.py:119
  6.7 4.9 %collective-permute-start = (f32[8,8,1,1024]{3,1,2,0:T(8,128)}, f32[8,8,1,1024]{3,1,2,0:T(8,128)S(1)}, u32[]{:S(2)}, u32[]{:S(2)}) collective-permute-start(f32[8,8,1,1024]{3,1,2,0:T(8,128)} %get-tuple-element.51), channel_id=1, source_target_pairs={{16,0},{32,16},{48,32},{64,48},{80,64},{96,80},{112,96},{0,112},{1... | collective-permute-start | bytes 786440 | tf_op jit(solution)/shard_map/ppermute | solution.py:37
  17.1 4.4 %fusion.125 = (f32[8,7,16,1024]{3,1,2,0:T(8,128)}, f32[8,7,16,1024]{3,1,2,0:T(8,128)}) fusion(f32[8,8,16,1024]{3,1,2,0:T(8,128)S(1)} %fusion.41), kind=kLoop, calls=%fused_computation.156 | loop fusion | bytes 14680064 | tf_op jit(solution)/shard_map/slice | solution.py:77
  21.6 10.0 %fusion.79 = f32[1,8,8]{2,1,0:T(8,128)S(1)} fusion(f32[8,8,16,1024]{3,1,2,0:T(8,128)S(1)} %fusion.41), kind=kOutput, calls=%fused_computation.103 | convolution fusion | flops 100663296 | bytes 4194560 | tf_op jit(solution)/shard_map/dot_general | solution.py:85
  35.3 13.6 %broadcast_multiply_fusion = (f32[8,8,16,1024]{3,1,2,0:T(8,128)S(1)}, f32[8,8,16,1024]{3,1,2,0:T(8,128)S(1)}) fusion(f32[8,7,16,1024]{3,1,2,0:T(8,128)} %get-tuple-element.53, f32[8,7,16,1024]{3,1,2,0:T(8,128)} %get-tuple-element.52, f32[8,8,1,1024]{3,1,2,0:T(8,128)S(1)} %collective-permute-done, f32[8,8,16,1024]{3,1,2,0:T(8,128)} %copy-done, ...), kind=kLoop, calls=%fused_computation.95 | loop fusion | flops 23068672 | bytes 20979712 | tf_op jit(solution)/shard_map/div | solution.py:79
  49.0 11.7 %fusion.82 = f32[1,8,8]{2,1,0:T(8,128)S(1)} fusion(f32[8,8,16,1024]{3,1,2,0:T(8,128)S(1)} %get-tuple-element.28, f32[8,8,16,1024]{3,1,2,0:T(8,128)S(1)} %copy-done.1), kind=kOutput, calls=%fused_computation.104 | convolution fusion | flops 100663296 | bytes 8388864 | tf_op jit(solution)/shard_map/dot_general | solution.py:85
  60.9 4.4 %fusion.120 = (f32[8,7,16,1024]{3,1,2,0:T(8,128)}, f32[8,7,16,1024]{3,1,2,0:T(8,128)}) fusion(f32[8,8,16,1024]{3,1,2,0:T(8,128)S(1)} %get-tuple-element.28), kind=kLoop, calls=%fused_computation.151 | loop fusion | bytes 14680064 | tf_op jit(solution)/shard_map/slice | solution.py:77
  69.6 10.0 %fusion.60 = f32[1,8,8]{2,1,0:T(8,128)S(1)} fusion(f32[8,8,16,1024]{3,1,2,0:T(8,128)S(1)} %get-tuple-element.28), kind=kOutput, calls=%fused_computation.98 | convolution fusion | flops 100663296 | bytes 4194560 | tf_op jit(solution)/shard_map/dot_general | solution.py:85
  79.6 8.0 %collective-permute-done.6 = f32[8,8,16,1]{3,1,2,0:T(8,128)S(1)} collective-permute-done((f32[8,8,16,1]{3,1,2,0:T(8,128)S(1)}, f32[8,8,16,1]{3,1,2,0:T(8,128)S(1)}, u32[]{:S(2)}, u32[]{:S(2)}) %collective-permute-start.6) | collective-permute-done | bytes 4128 | tf_op jit(solution)/shard_map/ppermute | solution.py:37
  88.5 9.2 %fusion.26 = f32[8,8,16,1024]{3,1,2,0:T(8,128)S(1)} fusion(f32[8,8,16,1]{3,1,2,0:T(8,128)S(1)} %collective-permute-done.7, f32[8,8,1,1024]{3,1,2,0:T(8,128)S(1)} %collective-permute-done.4, f32[8,8,16,1024]{3,1,2,0:T(8,128)S(1)} %get-tuple-element.28, f32[8,8,1,1024]{3,1,2,0:T(8,128)} %copy-done.7, f32[8,8,16,1]{3,1,2,0:T(8,128)} %copy-done.4, ...), kind=kLoop, calls=%fused_computation.43 | loop fusion | flops 27262976 | bytes 25174016 | tf_op jit(solution)/shard_map/sub | solution.py:126
  97.7 11.7 %fusion.63 = f32[1,8,8]{2,1,0:T(8,128)S(1)} fusion(f32[8,8,16,1024]{3,1,2,0:T(8,128)S(1)} %fusion.26, f32[8,8,16,1024]{3,1,2,0:T(8,128)S(1)} %get-tuple-element.28), kind=kOutput, calls=%fused_computation.99 | convolution fusion | flops 100663296 | bytes 8388864 | tf_op jit(solution)/shard_map/dot_general | solution.py:85
  109.7 4.4 %fusion.117 = (f32[8,7,16,1024]{3,1,2,0:T(8,128)}, f32[8,7,16,1024]{3,1,2,0:T(8,128)}) fusion(f32[8,8,16,1024]{3,1,2,0:T(8,128)S(1)} %fusion.26), kind=kLoop, calls=%fused_computation.148 | loop fusion | bytes 14680064 | tf_op jit(solution)/shard_map/slice | solution.py:77
  117.5 10.0 %fusion.68 = f32[1,8,8]{2,1,0:T(8,128)S(1)} fusion(f32[8,8,16,1024]{3,1,2,0:T(8,128)S(1)} %fusion.26), kind=kOutput, calls=%fused_computation.100 | convolution fusion | flops 100663296 | bytes 4194560 | tf_op jit(solution)/shard_map/dot_general | solution.py:85
  135.1 6.8 %fusion.16 = f32[8,8,16,1024]{3,1,2,0:T(8,128)S(1)} fusion(f32[8,8,16,1]{3,1,2,0:T(8,128)S(1)} %collective-permute-done.11, f32[8,8,1,1024]{3,1,2,0:T(8,128)S(1)} %collective-permute-done.8, f32[8,8,16,1024]{3,1,2,0:T(8,128)S(1)} %fusion.26, f32[8,8,1,1024]{3,1,2,0:T(8,128)} %copy-done.6, f32[8,8,16,1]{3,1,2,0:T(8,128)S(1)} %collective-permute-done.10, ...), kind=kLoop, calls=%fused_computation.25 | loop fusion | flops 25165824 | bytes 20979712 | tf_op jit(solution)/shard_map/sub | solution.py:126
  141.9 11.7 %fusion.71 = f32[1,8,8]{2,1,0:T(8,128)S(1)} fusion(f32[8,8,16,1024]{3,1,2,0:T(8,128)S(1)} %fusion.16, f32[8,8,16,1024]{3,1,2,0:T(8,128)S(1)} %fusion.26), kind=kOutput, calls=%fused_computation.101 | convolution fusion | flops 100663296 | bytes 8388864 | tf_op jit(solution)/shard_map/dot_general | solution.py:85
  162.5 10.0 %fusion.76 = f32[1,8,8]{2,1,0:T(8,128)S(1)} fusion(f32[8,8,16,1024]{3,1,2,0:T(8,128)S(1)} %fusion.16), kind=kOutput, calls=%fused_computation.102 | convolution fusion | flops 100663296 | bytes 4194560 | tf_op jit(solution)/shard_map/dot_general | solution.py:85
  178.7 7.1 %fusion.6 = f32[8,8,16,1024]{3,1,2,0:T(8,128)S(1)} fusion(f32[8,8,16,1024]{3,1,2,0:T(8,128)S(1)} %fusion.26, f32[8,8,16,1]{3,1,2,0:T(8,128)S(1)} %collective-permute-done.15, f32[8,8,1,1024]{3,1,2,0:T(8,128)S(1)} %collective-permute-done.12, f32[8,8,16,1024]{3,1,2,0:T(8,128)S(1)} %fusion.16, f32[8,8,1,1024]{3,1,2,0:T(8,128)} %copy-done.5, ...), kind=kLoop, calls=%fused_computation.7 | loop fusion | flops 24117248 | bytes 20979712 | tf_op jit(solution)/shard_map/sub | solution.py:126
  185.8 11.7 %fusion.87 = f32[1,8,8]{2,1,0:T(8,128)S(1)} fusion(f32[8,8,16,1024]{3,1,2,0:T(8,128)S(1)} %fusion.6, f32[8,8,16,1024]{3,1,2,0:T(8,128)S(1)} %fusion.16), kind=kOutput, calls=%fused_computation.105 | convolution fusion | flops 100663296 | bytes 8388864 | tf_op jit(solution)/shard_map/dot_general | solution.py:85
  197.5 6.5 %all-reduce.20 = (f32[2,8,8]{2,1,0:T(8,128)S(1)}, f32[2,8,8]{2,1,0:T(8,128)S(1)}, f32[2,8,8]{2,1,0:T(8,128)S(1)}, f32[2,8,8]{2,1,0:T(8,128)S(1)}) all-reduce(f32[2,8,8]{2,1,0:T(8,128)S(1)} %pad_maximum_fusion.25, f32[2,8,8]{2,1,0:T(8,128)S(1)} %pad_maximum_fusion.26, ...), channel_id=1, replica_groups=mesh['gx_0'=2,'gx_1'=4,'gy_0'=4,'gy_1'=2,'gy_2'=2] {'gx_0'}, use_global_device_ids=true, to_apply=%region_0.1 | all-reduce | flops 512 | bytes 4096 | tf_op jit(solution)/shard_map/psum | solution.py:25
  204.0 11.6 %all-reduce.17 = (f32[2,8,8]{2,1,0:T(8,128)S(1)}, f32[2,8,8]{2,1,0:T(8,128)S(1)}, f32[2,8,8]{2,1,0:T(8,128)S(1)}, f32[2,8,8]{2,1,0:T(8,128)S(1)}) all-reduce(f32[2,8,8]{2,1,0:T(8,128)S(1)} %get-tuple-element.22, f32[2,8,8]{2,1,0:T(8,128)S(1)} %get-tuple-element.23, ...), channel_id=1, replica_groups=mesh['gx_0'=2,'gx_1'=4,'gy_0'=4,'gy_1'=2,'gy_2'=2] {'gx_1'}, use_global_device_ids=true, to_apply=%region_1.2 | all-reduce | flops 512 | bytes 4096 | tf_op jit(solution)/shard_map/psum | solution.py:25
  215.6 13.6 %all-reduce.16 = (f32[2,8,8]{2,1,0:T(8,128)S(1)}, f32[2,8,8]{2,1,0:T(8,128)S(1)}, f32[2,8,8]{2,1,0:T(8,128)S(1)}, f32[2,8,8]{2,1,0:T(8,128)S(1)}) all-reduce(f32[2,8,8]{2,1,0:T(8,128)S(1)} %get-tuple-element.10, f32[2,8,8]{2,1,0:T(8,128)S(1)} %get-tuple-element.11, ...), channel_id=1, replica_groups=mesh['gx_0'=2,'gx_1'=4,'gy_0'=4,'gy_1'=2,'gy_2'=2] {'gy_0'}, use_global_device_ids=true, to_apply=%region_2.3 | all-reduce | flops 512 | bytes 4096 | tf_op jit(solution)/shard_map/psum | solution.py:25
  229.2 6.9 %all-reduce.19 = (f32[2,8,8]{2,1,0:T(8,128)S(1)}, f32[2,8,8]{2,1,0:T(8,128)S(1)}, f32[2,8,8]{2,1,0:T(8,128)S(1)}, f32[2,8,8]{2,1,0:T(8,128)S(1)}) all-reduce(f32[2,8,8]{2,1,0:T(8,128)S(1)} %get-tuple-element.6, f32[2,8,8]{2,1,0:T(8,128)S(1)} %get-tuple-element.7, ...), channel_id=1, replica_groups=mesh['gx_0'=2,'gx_1'=4,'gy_0'=4,'gy_1'=2,'gy_2'=2] {'gy_1'}, use_global_device_ids=true, to_apply=%region_3.4 | all-reduce | flops 512 | bytes 4096 | tf_op jit(solution)/shard_map/psum | solution.py:25
  236.1 19.1 %all-reduce.18 = (f32[2,8,8]{2,1,0:T(8,128)S(1)}, f32[2,8,8]{2,1,0:T(8,128)S(1)}, f32[2,8,8]{2,1,0:T(8,128)S(1)}, f32[2,8,8]{2,1,0:T(8,128)S(1)}) all-reduce(f32[2,8,8]{2,1,0:T(8,128)S(1)} %get-tuple-element.18, f32[2,8,8]{2,1,0:T(8,128)S(1)} %get-tuple-element.19, ...), channel_id=1, replica_groups=mesh['gx_0'=2,'gx_1'=4,'gy_0'=4,'gy_1'=2,'gy_2'=2] {'gy_2'}, use_global_device_ids=true, to_apply=%region_4.5 | all-reduce | flops 512 | bytes 4096 | tf_op jit(solution)/shard_map/psum | solution.py:25
  256.7 6.7 %copy.60 = f32[8,8,16,1024]{3,2,1,0:T(8,128)} copy(f32[8,8,16,1024]{3,1,2,0:T(8,128)} %copy-done.2) | data formatting | bytes 8388608
  (80 shorter events, 43.8 us)
Async XLA Ops:
  5.8 15.8 %copy-start = (f32[8,8,16,1024]{3,1,2,0:T(8,128)}, f32[8,8,16,1024]{3,1,2,0:T(8,128)S(1)}, u32[]{:S(2)}) copy-start(f32[8,8,16,1024]{3,1,2,0:T(8,128)S(1)} %fusion.41) | copy-start | bytes 12582916
  6.7 28.6 %collective-permute-start = (f32[8,8,1,1024]{3,1,2,0:T(8,128)}, f32[8,8,1,1024]{3,1,2,0:T(8,128)S(1)}, u32[]{:S(2)}, u32[]{:S(2)}) collective-permute-start(f32[8,8,1,1024]{3,1,2,0:T(8,128)} %get-tuple-element.51), channel_id=1, source_target_pairs={{16,0},{32,16},{48,32},{64,48},{80,64},{96,80},{112,96},{0,112},{1... | collective-permute-start | bytes 786440 | tf_op jit(solution)/shard_map/ppermute | solution.py:37
  11.7 23.7 %collective-permute-start.1 = (f32[8,8,1,1024]{3,1,2,0:T(8,128)}, f32[8,8,1,1024]{3,1,2,0:T(8,128)}, u32[]{:S(2)}, u32[]{:S(2)}) collective-permute-start(f32[8,8,1,1024]{3,1,2,0:T(8,128)} %get-tuple-element.50), channel_id=1, source_target_pairs={{0,16},{16,32},{32,48},{48,64},{64,80},{80,96},{96,112},{112,0},{1... | collective-permute-start | bytes 786440 | tf_op jit(solution)/shard_map/ppermute | solution.py:36
  12.8 19.8 %collective-permute-start.3 = (f32[8,8,16,1]{3,1,2,0:T(8,128)}, f32[8,8,16,1]{3,1,2,0:T(8,128)S(1)}, u32[]{:S(2)}, u32[]{:S(2)}) collective-permute-start(f32[8,8,16,1]{3,1,2,0:T(8,128)} %get-tuple-element.49), channel_id=1, source_target_pairs={{0,1},{1,2},{2,3},{3,4},{4,5},{5,6},{6,7},{7,8},{8,9},{9,10},{10,1... | collective-permute-start | bytes 12296 | tf_op jit(solution)/shard_map/ppermute | solution.py:36
  17.0 18.4 %collective-permute-start.2 = (f32[8,8,16,1]{3,1,2,0:T(8,128)}, f32[8,8,16,1]{3,1,2,0:T(8,128)}, u32[]{:S(2)}, u32[]{:S(2)}) collective-permute-start(f32[8,8,16,1]{3,1,2,0:T(8,128)} %get-tuple-element.48), channel_id=1, source_target_pairs={{1,0},{2,1},{3,2},{4,3},{5,4},{6,5},{7,6},{8,7},{9,8},{10,9},{11,1... | collective-permute-start | bytes 12296 | tf_op jit(solution)/shard_map/ppermute | solution.py:37
  21.6 10.0 %copy-start.3 = (s32[8,16,1024]{2,1,0:T(8,128)S(1)}, s32[8,16,1024]{2,1,0:T(8,128)}, u32[]{:S(2)}) copy-start(s32[8,16,1024]{2,1,0:T(8,128)} %param.3) | copy-start | bytes 1572868
  35.3 13.6 %copy-start.1 = (f32[8,8,16,1024]{3,1,2,0:T(8,128)S(1)}, f32[8,8,16,1024]{3,1,2,0:T(8,128)}, u32[]{:S(2)}) copy-start(f32[8,8,16,1024]{3,1,2,0:T(8,128)} %copy-done) | copy-start | bytes 12582916
  65.4 14.2 %collective-permute-start.7 = (f32[8,8,16,1]{3,1,2,0:T(8,128)S(1)}, f32[8,8,16,1]{3,1,2,0:T(8,128)S(1)}, u32[]{:S(2)}, u32[]{:S(2)}) collective-permute-start(f32[8,8,16,1]{3,1,2,0:T(8,128)S(1)} %get-tuple-element.45), channel_id=1, source_target_pairs={{0,1},{1,2},{2,3},{3,4},{4,5},{5,6},{6,7},{7,8},{8,9},{9,10},{10,1... | collective-permute-start | bytes 12296 | tf_op jit(solution)/shard_map/ppermute | solution.py:36
  65.9 21.7 %collective-permute-start.4 = (f32[8,8,1,1024]{3,1,2,0:T(8,128)S(1)}, f32[8,8,1,1024]{3,1,2,0:T(8,128)S(1)}, u32[]{:S(2)}, u32[]{:S(2)}) collective-permute-start(f32[8,8,1,1024]{3,1,2,0:T(8,128)S(1)} %get-tuple-element.47), channel_id=1, source_target_pairs={{16,0},{32,16},{48,32},{64,48},{80,64},{96,80},{112,96},{0,112},{1... | collective-permute-start | bytes 786440 | tf_op jit(solution)/shard_map/ppermute | solution.py:37
  69.2 18.4 %collective-permute-start.5 = (f32[8,8,1,1024]{3,1,2,0:T(8,128)S(1)}, f32[8,8,1,1024]{3,1,2,0:T(8,128)S(1)}, u32[]{:S(2)}, u32[]{:S(2)}) collective-permute-start(f32[8,8,1,1024]{3,1,2,0:T(8,128)S(1)} %get-tuple-element.46), channel_id=1, source_target_pairs={{0,16},{16,32},{32,48},{48,64},{64,80},{80,96},{96,112},{112,0},{1... | collective-permute-start | bytes 786440 | tf_op jit(solution)/shard_map/ppermute | solution.py:36
  69.2 18.4 %collective-permute-start.6 = (f32[8,8,16,1]{3,1,2,0:T(8,128)S(1)}, f32[8,8,16,1]{3,1,2,0:T(8,128)S(1)}, u32[]{:S(2)}, u32[]{:S(2)}) collective-permute-start(f32[8,8,16,1]{3,1,2,0:T(8,128)S(1)} %get-tuple-element.44), channel_id=1, source_target_pairs={{1,0},{2,1},{3,2},{4,3},{5,4},{6,5},{7,6},{8,7},{9,8},{10,9},{11,1... | collective-permute-start | bytes 12296 | tf_op jit(solution)/shard_map/ppermute | solution.py:37
  87.6 0.8 copy-start.4
  87.6 0.9 copy-start.7
  114.1 17.4 %collective-permute-start.11 = (f32[8,8,16,1]{3,1,2,0:T(8,128)S(1)}, f32[8,8,16,1]{3,1,2,0:T(8,128)S(1)}, u32[]{:S(2)}, u32[]{:S(2)}) collective-permute-start(f32[8,8,16,1]{3,1,2,0:T(8,128)S(1)} %get-tuple-element.39), channel_id=1, source_target_pairs={{0,1},{1,2},{2,3},{3,4},{4,5},{5,6},{6,7},{7,8},{8,9},{9,10},{10,1... | collective-permute-start | bytes 12296 | tf_op jit(solution)/shard_map/ppermute | solution.py:36
  114.1 20.2 %collective-permute-start.8 = (f32[8,8,1,1024]{3,1,2,0:T(8,128)S(1)}, f32[8,8,1,1024]{3,1,2,0:T(8,128)S(1)}, u32[]{:S(2)}, u32[]{:S(2)}) collective-permute-start(f32[8,8,1,1024]{3,1,2,0:T(8,128)S(1)} %get-tuple-element.41), channel_id=1, source_target_pairs={{16,0},{32,16},{48,32},{64,48},{80,64},{96,80},{112,96},{0,112},{1... | collective-permute-start | bytes 786440 | tf_op jit(solution)/shard_map/ppermute | solution.py:37
  117.0 17.3 %collective-permute-start.9 = (f32[8,8,1,1024]{3,1,2,0:T(8,128)S(1)}, f32[8,8,1,1024]{3,1,2,0:T(8,128)S(1)}, u32[]{:S(2)}, u32[]{:S(2)}) collective-permute-start(f32[8,8,1,1024]{3,1,2,0:T(8,128)S(1)} %get-tuple-element.40), channel_id=1, source_target_pairs={{0,16},{16,32},{32,48},{48,64},{64,80},{80,96},{96,112},{112,0},{1... | collective-permute-start | bytes 786440 | tf_op jit(solution)/shard_map/ppermute | solution.py:36
  117.0 17.3 %collective-permute-start.10 = (f32[8,8,16,1]{3,1,2,0:T(8,128)S(1)}, f32[8,8,16,1]{3,1,2,0:T(8,128)S(1)}, u32[]{:S(2)}, u32[]{:S(2)}) collective-permute-start(f32[8,8,16,1]{3,1,2,0:T(8,128)S(1)} %get-tuple-element.38), channel_id=1, source_target_pairs={{1,0},{2,1},{3,2},{4,3},{5,4},{6,5},{7,6},{8,7},{9,8},{10,9},{11,1... | collective-permute-start | bytes 12296 | tf_op jit(solution)/shard_map/ppermute | solution.py:37
  134.4 0.7 copy-start.6
  158.3 18.5 %collective-permute-start.15 = (f32[8,8,16,1]{3,1,2,0:T(8,128)S(1)}, f32[8,8,16,1]{3,1,2,0:T(8,128)S(1)}, u32[]{:S(2)}, u32[]{:S(2)}) collective-permute-start(f32[8,8,16,1]{3,1,2,0:T(8,128)S(1)} %get-tuple-element.33), channel_id=1, source_target_pairs={{0,1},{1,2},{2,3},{3,4},{4,5},{5,6},{6,7},{7,8},{8,9},{9,10},{10,1... | collective-permute-start | bytes 12296 | tf_op jit(solution)/shard_map/ppermute | solution.py:36
  159.5 18.5 %collective-permute-start.12 = (f32[8,8,1,1024]{3,1,2,0:T(8,128)S(1)}, f32[8,8,1,1024]{3,1,2,0:T(8,128)S(1)}, u32[]{:S(2)}, u32[]{:S(2)}) collective-permute-start(f32[8,8,1,1024]{3,1,2,0:T(8,128)S(1)} %get-tuple-element.35), channel_id=1, source_target_pairs={{16,0},{32,16},{48,32},{64,48},{80,64},{96,80},{112,96},{0,112},{1... | collective-permute-start | bytes 786440 | tf_op jit(solution)/shard_map/ppermute | solution.py:37
  162.5 15.5 %collective-permute-start.13 = (f32[8,8,1,1024]{3,1,2,0:T(8,128)S(1)}, f32[8,8,1,1024]{3,1,2,0:T(8,128)S(1)}, u32[]{:S(2)}, u32[]{:S(2)}) collective-permute-start(f32[8,8,1,1024]{3,1,2,0:T(8,128)S(1)} %get-tuple-element.34), channel_id=1, source_target_pairs={{0,16},{16,32},{32,48},{48,64},{64,80},{80,96},{96,112},{112,0},{1... | collective-permute-start | bytes 786440 | tf_op jit(solution)/shard_map/ppermute | solution.py:36
  162.5 15.5 %collective-permute-start.14 = (f32[8,8,16,1]{3,1,2,0:T(8,128)S(1)}, f32[8,8,16,1]{3,1,2,0:T(8,128)S(1)}, u32[]{:S(2)}, u32[]{:S(2)}) collective-permute-start(f32[8,8,16,1]{3,1,2,0:T(8,128)S(1)} %get-tuple-element.32), channel_id=1, source_target_pairs={{1,0},{2,1},{3,2},{4,3},{5,4},{6,5},{7,6},{8,7},{9,8},{10,9},{11,1... | collective-permute-start | bytes 12296 | tf_op jit(solution)/shard_map/ppermute | solution.py:37
  185.8 11.7 %copy-start.2 = (f32[8,8,16,1024]{3,1,2,0:T(8,128)}, f32[8,8,16,1024]{3,1,2,0:T(8,128)S(1)}, u32[]{:S(2)}) copy-start(f32[8,8,16,1024]{3,1,2,0:T(8,128)S(1)} %fusion.6) | copy-start | bytes 12582916
  185.8 70.2 %copy-start.8 = (f32[8]{0:T(128)S(1)}, f32[8]{0:T(128)}, u32[]{:S(2)}) copy-start(f32[8]{0:T(128)} %constant.126) | copy-start | bytes 100
  (1 other events, 0.7 us)
where the time goes:
time: 269 us; the launch traced here: 264 us
  matrix products  87.3 us (32%)
  blocking collectives  57.7 us (21%)
  other arithmetic  42.9 us (16%)
  local copies, waits for them, and re-layouts  31 us (12%)
  waiting for transfers between devices  23.2 us (9%)
  starting transfers between devices  20.9 us (8%)
    dot_general x8, matrix products, inner_matrix(): jnp.dot(left, right.T, precision=lax.Precision.HIGHEST, preferred_element...  86.6 us
    psum x5, blocking collectives, one_axis_at_a_time(): return functools.reduce(lax.psum, axes, array)  57.7 us
    sub x3, other arithmetic, on_device(): vectors.append(2.0 * hopped - vectors[-2])  23.1 us
    slice x4, local copies, waits for them, and re-layouts, hopping(): beside = beside + jnp.concatenate([center[:, 1:], zeros_plane], 1)  17.8 us
    ppermute x8, starting transfers between devices, extended(): lax.ppermute(first, axis, [(b, a) for a, b in up])  15.1 us
    ppermute x8, waiting for transfers between devices, extended(): lax.ppermute(first, axis, [(b, a) for a, b in up])  14.8 us
    div x1, other arithmetic, hopping(): return (onsite[None] * center - beside) / spectral_scale  13.6 us
    unnamed x19, local copies, waits for them, and re-layouts  9.04 us
  transfers between devices with their start and end apart: 16, of which 6 were waited for; matrix products, arithmetic and copies ran while one was open for 18% of the time, Pallas kernels for 0%

commit v1 on v0

v1 whole, which is shorter than its diff:
```python
import functools
import math

import jax
import jax.numpy as jnp
import numpy as np
from jax import lax
from jax.experimental import pallas as pl
from jax.experimental.pallas import tpu as pltpu
from jax.sharding import PartitionSpec as P

PROBES = 8
PL = 8
STEPS = 4
LEVELS = 8
NE = 8192
NMOM = 8
NX = 128
NY = 16384
SITES = 16777216
GXN = 8
GYN = 16
ROWS = NX // GXN
COLS = NY // GYN
TILES = COLS // 128
EB = NE // (GXN * GYN)
SPAN = PL + 1
GROUP = 4

disorder_width = 4.0
field_strength = 3.0
spectral_scale = 10.0
energy_edge = 0.9

MESH = pl.DeviceIdType.MESH
F32 = jnp.float32
BF16 = jnp.bfloat16


def energy_tables():
    theta = np.arccos(energy_edge * np.cos(math.pi * (np.arange(NE) + 0.5) / NE))
    total = NMOM + 1.0
    rows = []
    for m in range(NMOM):
        damp = (
            (NMOM - m + 1.0) * math.cos(math.pi * m / total)
            + math.sin(math.pi * m / total) / math.tan(math.pi / total)
        ) / total
        weight = damp if m == 0 else 2.0 * damp
        rows.append(
            np.stack(
                [
                    -weight * np.sin(m * theta) / np.sin(theta),
                    -weight * np.cos(m * theta) / np.sin(theta),
                ]
            )
        )
    table = np.stack(rows).reshape(NMOM, 2, GXN * GYN, EB)
    return np.ascontiguousarray(table.transpose(2, 0, 1, 3).reshape(GXN * GYN, NMOM, 2 * EB)).astype(np.float32)


def lanes():
    return lax.broadcasted_iota(jnp.int32, (8, 128), 1)


def split(pair):
    high = pair.astype(BF16)
    return high, (pair - high.astype(F32)).astype(BF16)


def main_kernel(
    levels, bits, last, moments_out,
    field, raw, halves, onsite, lev, edge_out, edge_in, grams, flat, first, second,
    row_send, row_recv, col_send, col_recv, load_sem, lev_sem, sum_send, sum_recv,
):
    gx, gy = lax.axis_index("gx"), lax.axis_index("gy")
    up, down = (lax.rem(gx + GXN - 1, GXN), gy), (lax.rem(gx + 1, GXN), gy)
    left, right = (gx, lax.rem(gy + GYN - 1, GYN)), (gx, lax.rem(gy + 1, GYN))

    def row_copy(n, p, side):
        target = (up, down)[side]
        here, there = ((1, ROWS + 1), (ROWS, 0))[side]
        if n == 0:
            src, dst = bits.at[:, p, here - 1, :], raw.at[p, there]
        else:
            src, dst = field.at[n * SPAN + 1 + p, here], field.at[n * SPAN + 1 + p, there]
        return pltpu.make_async_remote_copy(
            src, dst, row_send.at[n, side, p], row_recv.at[n, side, p],
            device_id=target, device_id_type=MESH,
        )

    def col_copy(n, p, side):
        return pltpu.make_async_remote_copy(
            edge_out.at[n, side, p], edge_in.at[n, side, p],
            col_send.at[n, side, p], col_recv.at[n, side, p],
            device_id=(left, right)[side], device_id_type=MESH,
        )

    def load(p, i):
        return pltpu.make_async_copy(bits.at[i, p], raw.at[p, pl.ds(1, ROWS), i, :], load_sem.at[p, i])

    barrier = pltpu.get_barrier_semaphore()
    for d in range(1, GXN):
        pl.semaphore_signal(barrier, inc=1, device_id=(lax.rem(gx + d, GXN), gy), device_id_type=MESH)
    for d in range(1, GYN):
        pl.semaphore_signal(barrier, inc=1, device_id=(gx, lax.rem(gy + d, GYN)), device_id_type=MESH)

    lev_copy = pltpu.make_async_copy(levels, lev, lev_sem)
    lev_copy.start()

    @pl.loop(0, PL)
    def _(p):
        for i in range(PROBES):
            load(p, i).start()

    pl.semaphore_wait(barrier, GXN + GYN - 2)

    @pl.loop(0, PL)
    def _(p):
        for side in range(2):
            row_copy(0, p, side).start()

    @pl.loop(0, STEPS + 1)
    def _(n):
        field[n * SPAN] = jnp.zeros((ROWS + 2, PROBES, COLS), F32)

    grams[...] = jnp.zeros_like(grams)
    flat[...] = jnp.zeros_like(flat)
    lev_copy.wait()

    @pl.loop(0, PL)
    def _(p):
        for i in range(PROBES):
            load(p, i).wait()

        def rows(g, edges):
            left_edge, right_edge = edges
            lane = lanes()
            for k in range(0, GROUP, 2):
                x = g * GROUP + k
                at = pl.multiple_of(x * PROBES, 16)
                for c in range(TILES):
                    cut = pl.ds(c * 128, 128)
                    pair = []
                    for q in (0, 1):
                        value = (2 * raw[p, x + q + 1, :, cut] - 1).astype(F32)
                        field[p + 1, x + q + 1, :, cut] = value
                        pair.append(value)
                        if c == 0:
                            left_edge = jnp.where(lane == x + q, pltpu.roll(value, x + q, 1), left_edge)
                        if c == TILES - 1:
                            right_edge = jnp.where(lane == x + q, pltpu.roll(value, x + q + 1, 1), right_edge)
                    halves[0, p, pl.ds(at, 16), cut] = jnp.concatenate(pair, 0).astype(BF16)
            return left_edge, right_edge

        zero = jnp.zeros((8, 128), F32)
        left_edge, right_edge = lax.fori_loop(0, ROWS // GROUP, rows, (zero, zero))
        edge_out[0, 0, p] = left_edge
        edge_out[0, 1, p] = right_edge
        for side in range(2):
            col_copy(0, p, side).start()
        for x in range(ROWS):
            row = (gx * ROWS + x).astype(F32)
            slope = field_strength * ((row + 0.5) / NX - 0.5)
            value = disorder_width * (lev[p, pl.ds(x, 1), :].astype(F32) / (LEVELS - 1) - 0.5) + slope
            onsite[p, x] = jnp.broadcast_to(value, (PROBES, COLS))

    def step(n, p):
        base = n * SPAN + 1 + p
        for side in range(2):
            row_copy(n, p, side).wait_recv()
            col_copy(n, p, side).wait_recv()
        if n == 0:
            for x in (0, ROWS + 1):
                field[base, x] = (2 * raw[p, x] - 1).astype(F32)
        from_right, from_left = edge_in[n, 0, p], edge_in[n, 1, p]

        def rows(g, edges):
            left_edge, right_edge = edges
            lane = lanes()
            is_first, is_last = lane == 0, lane == 127
            x0 = g * GROUP

            def column(c):
                return [field[base, x0 + k, :, pl.ds(c * 128, 128)] for k in range(GROUP + 2)]

            own = range(1, GROUP + 1)
            before = [pltpu.roll(from_left, lax.rem(128 - (x0 + k - 1), 128), 1) for k in own]
            beyond = [pltpu.roll(from_right, 127 - (x0 + k - 1), 1) for k in own]
            now = column(0)
            forth = [pltpu.roll(now[k], 1, 1) for k in own]
            back = [pltpu.roll(now[k], 127, 1) for k in own]
            for c in range(TILES):
                cut = pl.ds(c * 128, 128)
                if c + 1 < TILES:
                    later = column(c + 1)
                    later_forth = [pltpu.roll(later[k], 1, 1) for k in own]
                    later_back = [pltpu.roll(later[k], 127, 1) for k in own]
                else:
                    later, later_forth, later_back = None, None, beyond
                made = []
                for k in own:
                    x = x0 + k - 1
                    beside = now[k + 1] + now[k - 1]
                    beside = beside + jnp.where(is_last, later_back[k - 1], back[k - 1])
                    beside = beside + jnp.where(is_first, before[k - 1], forth[k - 1])
                    beside = beside + field[base + 1, x + 1, :, cut]
                    beside = beside + field[base - 1, x + 1, :, cut]
                    hopped = onsite[p, x, :, cut] * now[k] - beside
                    if n == 0:
                        value = hopped * (1.0 / spectral_scale)
                    else:
                        value = hopped * (2.0 / spectral_scale) - field[base - SPAN, x + 1, :, cut]
                    if n + 1 < STEPS:
                        field[base + SPAN, x + 1, :, cut] = value
                        if c == 0:
                            left_edge = jnp.where(lane == x, pltpu.roll(value, x, 1), left_edge)
                        if c == TILES - 1:
                            right_edge = jnp.where(lane == x, pltpu.roll(value, x + 1, 1), right_edge)
                    else:
                        last[p, x, :, cut] = value
                    made.append(value)
                for k in range(0, GROUP, 2):
                    high, low = split(jnp.concatenate(made[k : k + 2], 0))
                    at = pl.multiple_of((x0 + k) * PROBES, 16)
                    halves[(n + 1) % 2, p, pl.ds(at, 16), cut] = high
                    halves[(n + 1) % 2, p, pl.ds(ROWS * PROBES + at, 16), cut] = low
                now, before, forth, back = later, forth, later_forth, later_back
            return left_edge, right_edge

        zero = jnp.zeros((8, 128), F32)
        left_edge, right_edge = lax.fori_loop(0, ROWS // GROUP, rows, (zero, zero))
        if n + 1 < STEPS:
            edge_out[n + 1, 0, p] = left_edge
            edge_out[n + 1, 1, p] = right_edge
            for side in range(2):
                row_copy(n + 1, p, side).start()
                col_copy(n + 1, p, side).start()

        lane_group = lanes() // PROBES
        held = ROWS * PROBES if n == 0 else 2 * ROWS * PROBES
        stays = halves[n % 2, p, 0:held]
        for which, other in ((0, stays), (1, halves[(n + 1) % 2, p])):
            product = lax.dot_general(stays, other, (((1,), (1,)), ((), ())), preferred_element_type=F32)
            total = None
            for part in range(0, product.shape[0], ROWS * PROBES):
                for c in range(0, product.shape[1], 128):
                    chosen = product[part : part + PROBES, c : c + 128]
                    for x in range(1, ROWS):
                        block = product[part + x * PROBES : part + (x + 1) * PROBES, c : c + 128]
                        chosen = jnp.where(lane_group == x, block, chosen)
                    total = chosen if total is None else total + chosen
            grams[2 * n + which] += total

    for n in range(STEPS):
        pl.loop(0, PL)(functools.partial(step, n))

    lane, sub = lanes(), lax.broadcasted_iota(jnp.int32, (8, 128), 0)
    keep = sub == lane // PROBES
    packed = jnp.zeros((8, 128), F32)
    for m in range(NMOM):
        total = grams[m]
        for shift in (8, 16, 32, 64):
            total = total + pltpu.roll(total, shift, 1)
        row = jnp.sum(jnp.where(keep, total, 0.0), axis=0, keepdims=True)
        packed = jnp.where(sub == m, jnp.broadcast_to(row, (8, 128)), packed)
    flat[...] = packed

    first[gy] = packed
    copies = []
    for d in range(1, GYN):
        c = pltpu.make_async_remote_copy(
            flat, first.at[gy], sum_send.at[0, d], sum_recv.at[0, d],
            device_id=(gx, lax.rem(gy + d, GYN)), device_id_type=MESH,
        )
        c.start()
        copies.append(c)
    for d in range(1, GYN):
        pltpu.make_async_remote_copy(
            flat, first.at[lax.rem(gy + GYN - d, GYN)], sum_send.at[0, d], sum_recv.at[0, d],
            device_id=(gx, lax.rem(gy + d, GYN)), device_id_type=MESH,
        ).wait_recv()
    total = first[0]
    for d in range(1, GYN):
        total = total + first[d]
    second[gx] = total
    for d in range(1, GXN):
        c = pltpu.make_async_remote_copy(
            second.at[gx], second.at[gx], sum_send.at[1, d], sum_recv.at[1, d],
            device_id=(lax.rem(gx + d, GXN), gy), device_id_type=MESH,
        )
        c.start()
        copies.append(c)
    for d in range(1, GXN):
        source = lax.rem(gx + GXN - d, GXN)
        pltpu.make_async_remote_copy(
            second.at[source], second.at[source], sum_send.at[1, d], sum_recv.at[1, d],
            device_id=(lax.rem(gx + d, GXN), gy), device_id_type=MESH,
        ).wait_recv()
    total = second[0]
    for d in range(1, GXN):
        total = total + second[d]
    moments_out[...] = total

    for c in copies:
        c.wait_send()
    for n in range(STEPS):

        @pl.loop(0, PL)
        def _(p):
            for side in range(2):
                row_copy(n, p, side).wait_send()
                col_copy(n, p, side).wait_send()


def finish_kernel(vector, grams, table, green, out, table_here, out_sem, table_sem):
    device = lax.axis_index("gx") * GYN + lax.axis_index("gy")
    fetch = pltpu.make_async_copy(table.at[device], table_here, table_sem)
    fetch.start()
    copies = []
    for p in range(PL):
        for i in range(PROBES):
            c = pltpu.make_async_copy(vector.at[p, :, i, :], out.at[i, p], out_sem.at[p, i])
            c.start()
            copies.append(c)
    fetch.wait()
    scaled = grams[...] / SITES
    rows = [scaled[0:1], scaled[1:2]]
    for m in range(2, NMOM):
        rows.append(2.0 * scaled[m : m + 1] - rows[m % 2])
    moments = jnp.concatenate(rows + [jnp.zeros((128 - NMOM, 128), F32)], 0)
    weights = jnp.transpose(jnp.concatenate([table_here[...], jnp.zeros((128 - NMOM, 128), F32)], 0))
    result = jnp.dot(weights, moments, precision=lax.Precision.HIGHEST, preferred_element_type=F32)
    green[0] = result[0:EB, 0 : PROBES * PROBES]
    green[1] = result[EB : 2 * EB, 0 : PROBES * PROBES]
    for c in copies:
        c.wait()


def on_device(levels, probe_bits):
    anywhere = pl.BlockSpec(memory_space=pl.ANY)
    vmem = pl.BlockSpec(memory_space=pltpu.VMEM)
    dma = pltpu.SemaphoreType.DMA
    last, grams = pl.pallas_call(
        main_kernel,
        out_shape=(
            pltpu.VMEM((PL, ROWS, PROBES, COLS), F32),
            pltpu.VMEM((8, 128), F32),
        ),
        in_specs=[anywhere, anywhere],
        out_specs=(vmem, vmem),
        scratch_shapes=[
            pltpu.VMEM((STEPS * SPAN + 1, ROWS + 2, PROBES, COLS), F32),
            pltpu.VMEM((PL, ROWS + 2, PROBES, COLS), jnp.int32),
            pltpu.VMEM((2, PL, 2 * ROWS * PROBES, COLS), BF16),
            pltpu.VMEM((PL, ROWS, PROBES, COLS), F32),
            pltpu.VMEM((PL, ROWS, COLS), jnp.int32),
            pltpu.VMEM((STEPS, 2, PL, 8, 128), F32),
            pltpu.VMEM((STEPS, 2, PL, 8, 128), F32),
            pltpu.VMEM((NMOM, 8, 128), F32),
            pltpu.VMEM((8, 128), F32),
            pltpu.VMEM((GYN, 8, 128), F32),
            pltpu.VMEM((GXN, 8, 128), F32),
            dma((STEPS, 2, PL)),
            dma((STEPS, 2, PL)),
            dma((STEPS, 2, PL)),
            dma((STEPS, 2, PL)),
            dma((PL, PROBES)),
            dma,
            dma((2, GYN)),
            dma((2, GYN)),
        ],
        compiler_params=pltpu.CompilerParams(
            collective_id=0, has_side_effects=True, vmem_limit_bytes=52 << 20
        ),
    )(levels, probe_bits)
    green, out = pl.pallas_call(
        finish_kernel,
        out_shape=(
            jax.ShapeDtypeStruct((2, EB, PROBES * PROBES), F32),
            jax.ShapeDtypeStruct((PROBES, PL, ROWS, COLS), F32),
        ),
        in_specs=[vmem, vmem, anywhere],
        out_specs=(vmem, anywhere),
        scratch_shapes=[
            pltpu.VMEM((NMOM, 2 * EB), F32),
            dma((PL, PROBES)),
            dma,
        ],
        compiler_params=pltpu.CompilerParams(vmem_limit_bytes=8 << 20),
    )(last, grams, jnp.asarray(energy_tables()))
    return green, out


def solution(mesh):
    return jax.shard_map(
        on_device,
        mesh=mesh,
        in_specs=(P(None, "gx", "gy"), P(None, None, "gx", "gy")),
        out_specs=(P(None, ("gx", "gy"), None), P(None, None, "gx", "gy")),
        check_vma=False,
    )
```

time: 269 us -> 69.2 us (0.26); the launches traced: 264 us -> 69.1 us
  matrix products: 87.3 us -> 0 us
  Pallas kernels: 0 us -> 68.4 us
  blocking collectives: 57.7 us -> 0 us
  other arithmetic: 42.9 us -> 0 us
  local copies, waits for them, and re-layouts: 31 us -> 0.01 us
  waiting for transfers between devices: 23.2 us -> 0 us
  starting transfers between devices: 20.9 us -> 0 us
    dot_general x10 -> x0, matrix products: 87.3 us -> none  [the longest x8 86.6 us: inner_matrix(): jnp.dot(left, right.T, precision=lax.Precision.HIGHEST, preferred_element...]
    pallas_call x0 -> x2, Pallas kernels: none -> 68.4 us  [the longest x1 65.3 us: on_device(): pl.pallas_call(main_kernel, out_shape=(pltpu.VMEM((PL, ROWS, PROBES, COLS...]
    psum x5 -> x0, blocking collectives: 57.7 us -> none  [one_axis_at_a_time(): return functools.reduce(lax.psum, axes, array)]
    ppermute x16 -> x0, waiting for transfers between devices: 23.2 us -> none  [the longest x8 14.8 us: extended(): lax.ppermute(first, axis, [(b, a) for a, b in up])]
    sub x4 -> x0, other arithmetic: 23.1 us -> none  [the longest x3 23.1 us: on_device(): vectors.append(2.0 * hopped - vectors[-2])]
    ppermute x16 -> x0, starting transfers between devices: 20.9 us -> none  [the longest x8 15.1 us: extended(): lax.ppermute(first, axis, [(b, a) for a, b in up])]
    slice x12 -> x0, local copies, waits for them, and re-layouts: 20.7 us -> none  [the longest x4 17.8 us: hopping(): beside = beside + jnp.concatenate([center[:, 1:], zeros_plane], 1)]
    div x1 -> x0, other arithmetic: 13.6 us -> none  [hopping(): return (onsite[None] * center - beside) / spectral_scale]
  transfers between devices with their start and end apart: 16 -> 0, of which waited for: 6 -> 0; matrix products, arithmetic and copies ran while one was open for 18% -> 0% of each run, Pallas kernels for 0% -> 0%
where the time goes in v1:
time: 69.2 us; the launch traced here: 69.1 us
  Pallas kernels  68.4 us (99%)
    pallas_call x1, Pallas kernels, on_device(): pl.pallas_call(main_kernel, out_shape=(pltpu.VMEM((PL, ROWS, PROBES, COLS...  65.3 us
    pallas_call x1, Pallas kernels, on_device(): pl.pallas_call(finish_kernel, out_shape=(jax.ShapeDtypeStruct((2, EB, PRO...  3.19 us

profile of v1, /device:TPU:1, one launch (start us, length us, event | category | flops | bytes accessed | tf_op | source)
XLA Modules:
  0.0 69.1 jit_solution(1194771473072077733)
XLA Ops:
  0.6 0.0 copy-start
  0.6 65.3 %shard_map.50 = (f32[8,16,8,1024]{3,2,1,0:T(8,128)S(1)}, f32[8,128]{1,0:T(8,128)S(1)}) custom-call(s32[8,16,1024]{2,1,0:T(8,128)} %levels.1, s32[8,8,16,1024]{3,2,1,0:T(8,128)} %bits.1), custom_call_target="tpu_custom_call" | custom-call | tf_op jit(solution)/shard_map/pallas_call | solution.py:344
  65.9 0.0 copy-done
  65.9 3.2 %shard_map.51 = (f32[2,64,64]{2,1,0:T(8,128)}, f32[8,8,16,1024]{3,2,1,0:T(8,128)}) custom-call(f32[8,16,8,1024]{3,2,1,0:T(8,128)S(1)} %get-tuple-element.4.vector, f32[8,128]{1,0:T(8,128)S(1)} %get-tuple-element.5.grams, f32[128,8,128]{2,1,0:T(8,128)S(1)} %copy-done), custom_call_target="tpu_custom_call" | custom-call | tf_op jit(solution)/shard_map/pallas_call | solution.py:377
Async XLA Ops:
  0.6 65.3 %copy-start = (f32[128,8,128]{2,1,0:T(8,128)S(1)}, f32[128,8,128]{2,1,0:T(8,128)}, u32[]{:S(2)}) copy-start(f32[128,8,128]{2,1,0:T(8,128)} %constant.2.clone.table) | copy-start | bytes 1572868

commit v2 on v1

v2 whole, which is shorter than its diff:
```python
import functools
import math

import jax
import jax.numpy as jnp
import numpy as np
from jax import lax
from jax.experimental import pallas as pl
from jax.experimental.pallas import tpu as pltpu
from jax.sharding import PartitionSpec as P

PROBES = 8
PL = 8
STEPS = 4
LEVELS = 8
NE = 8192
NMOM = 8
NX = 128
NY = 16384
SITES = 16777216
GXN = 8
GYN = 16
ROWS = NX // GXN
COLS = NY // GYN
TILES = COLS // 128
EB = NE // (GXN * GYN)
DEFER = 3
PART = ROWS * PROBES
HALF = 2 * PART
BLOCK = 256

disorder_width = 4.0
field_strength = 3.0
spectral_scale = 10.0
energy_edge = 0.9

MESH = pl.DeviceIdType.MESH
F32 = jnp.float32
BF16 = jnp.bfloat16


def energy_tables():
    theta = np.arccos(energy_edge * np.cos(math.pi * (np.arange(NE) + 0.5) / NE))
    total = NMOM + 1.0
    rows = []
    for m in range(NMOM):
        damp = (
            (NMOM - m + 1.0) * math.cos(math.pi * m / total)
            + math.sin(math.pi * m / total) / math.tan(math.pi / total)
        ) / total
        weight = damp if m == 0 else 2.0 * damp
        rows.append(
            np.stack(
                [
                    -weight * np.sin(m * theta) / np.sin(theta),
                    -weight * np.cos(m * theta) / np.sin(theta),
                ]
            )
        )
    table = np.stack(rows).reshape(NMOM, 2, GXN * GYN, EB)
    return np.ascontiguousarray(table.transpose(2, 0, 1, 3).reshape(GXN * GYN, NMOM, 2 * EB)).astype(np.float32)


def lanes():
    return lax.broadcasted_iota(jnp.int32, (8, 128), 1)


def split(pair):
    high = pair.astype(BF16)
    return high, (pair - high.astype(F32)).astype(BF16)


def main_kernel(
    levels, bits, last, moments_out,
    field0, field1, field2, field3, raw, halves, onsite, lev, mix, unmix,
    edge_out, edge_in, grams, flat, first, second,
    row_send, row_recv, col_send, col_recv, load_sem, lev_sem, sum_send, sum_recv,
):
    fields = (field0, field1, field2, field3)
    gx, gy = lax.axis_index("gx"), lax.axis_index("gy")
    up, down = (lax.rem(gx + GXN - 1, GXN), gy), (lax.rem(gx + 1, GXN), gy)
    left, right = (gx, lax.rem(gy + GYN - 1, GYN)), (gx, lax.rem(gy + 1, GYN))

    def row_copy(n, p, side):
        here, there = ((1, ROWS + 1), (ROWS, 0))[side]
        return pltpu.make_async_remote_copy(
            fields[n].at[p + 1, here], fields[n].at[p + 1, there],
            row_send.at[n, side, p], row_recv.at[n, side, p],
            device_id=(up, down)[side], device_id_type=MESH,
        )

    def col_copy(n, p, side):
        return pltpu.make_async_remote_copy(
            edge_out.at[n, side, p], edge_in.at[n, side, p],
            col_send.at[n, side, p], col_recv.at[n, side, p],
            device_id=(left, right)[side], device_id_type=MESH,
        )

    def send_rows(n, p):
        for side in range(2):
            row_copy(n, p, side).start()

    def send_edges(n, p, left_edge, right_edge):
        edge_out[n, 0, p] = left_edge
        edge_out[n, 1, p] = right_edge
        for side in range(2):
            col_copy(n, p, side).start()

    def load(p, i):
        return pltpu.make_async_copy(bits.at[i, p], raw.at[p, :, i, :], load_sem.at[p, i])

    barrier = pltpu.get_barrier_semaphore()
    for d in range(1, GXN):
        pl.semaphore_signal(barrier, inc=1, device_id=(lax.rem(gx + d, GXN), gy), device_id_type=MESH)
    for d in range(1, GYN):
        pl.semaphore_signal(barrier, inc=1, device_id=(gx, lax.rem(gy + d, GYN)), device_id_type=MESH)

    @pl.loop(0, PL)
    def _(p):
        for i in range(PROBES):
            load(p, i).start()

    lev_copy = pltpu.make_async_copy(levels, lev, lev_sem)
    lev_copy.start()

    source = lax.broadcasted_iota(jnp.int32, (BLOCK, BLOCK), 0)
    place = lax.broadcasted_iota(jnp.int32, (BLOCK, BLOCK), 1)
    mix[...] = jnp.where(source == lax.rem(place, 128) * 2 + place // 128, 1.0, 0.0).astype(BF16)
    unmix[...] = jnp.where(place == lax.rem(source, 128) * 2 + source // 128, 1.0, 0.0).astype(BF16)

    def moved(value, matrix):
        order = matrix[...]
        return jnp.concatenate(
            [
                lax.dot_general(
                    value[:, c : c + BLOCK], order, (((1,), (0,)), ((), ())), preferred_element_type=F32
                )
                for c in range(0, COLS, BLOCK)
            ],
            1,
        )

    def begin(p):
        for i in range(PROBES):
            load(p, i).wait()
        signs = (2 * raw[p] - 1).astype(F32).reshape(ROWS * PROBES, COLS)
        value = moved(signs.astype(BF16), mix)
        halves[p, 0 : ROWS * PROBES] = value.astype(BF16)
        left_edge, right_edge = jnp.zeros((8, 128), F32), jnp.zeros((8, 128), F32)
        lane = lanes()
        for x in range(ROWS):
            row = value[x * PROBES : (x + 1) * PROBES]
            field0[p + 1, x + 1] = row
            left_edge = jnp.where(lane == x, pltpu.roll(row[:, 0:128], x, 1), left_edge)
            right_edge = jnp.where(lane == x, pltpu.roll(row[:, COLS - 128 :], x + 1, 1), right_edge)
        return left_edge, right_edge

    pl.semaphore_wait(barrier, GXN + GYN - 2)

    @pl.loop(0, PL)
    def _(p):
        left_edge, right_edge = begin(p)
        send_edges(0, p, left_edge, right_edge)
        if DEFER == 0:
            send_rows(0, p)
        else:
            pl.when(p < PL - DEFER)(lambda: send_rows(0, p))

    for field in fields:
        for p in (0, PL + 1):

            @pl.loop(0, ROWS + 2)
            def _(x):
                field[p, x] = jnp.zeros((PROBES, COLS), F32)

    grams[...] = jnp.zeros_like(grams)

    lev_copy.wait()
    level = moved(lev[...].astype(F32).astype(BF16).reshape(PL * ROWS, COLS), mix)
    for x in range(ROWS):
        slope = field_strength * (((gx * ROWS + x).astype(F32) + 0.5) / NX - 0.5)
        for p in range(PL):
            at = p * ROWS + x
            value = disorder_width * (level[at : at + 1] / (LEVELS - 1) - 0.5) + slope
            onsite[p, x] = jnp.broadcast_to(value, (PROBES, COLS))

    def step(n, p):
        field, base = fields[n], p + 1
        older = fields[n - 1] if n else None
        newer = fields[n + 1] if n + 1 < STEPS else None
        kept, fresh = (n % 2) * HALF, ((n + 1) % 2) * HALF
        for side in range(2):
            col_copy(n, p, side).wait_recv()
            row_copy(n, p, side).wait_recv()
        from_right, from_left = edge_in[n, 0, p], edge_in[n, 1, p]
        left_edge, right_edge = jnp.zeros((8, 128), F32), jnp.zeros((8, 128), F32)
        lane = lanes()
        is_first, is_last = lane == 0, lane == 127

        def tiles(x):
            return [field[base, x, :, t * 128 : (t + 1) * 128] for t in range(TILES)]

        above, now = tiles(0), tiles(1)
        pair = []
        for x in range(ROWS):
            below = tiles(x + 2)
            forth = [pltpu.roll(from_left, (128 - x) % 128, 1)]
            forth += [pltpu.roll(now[t], 1, 1) for t in range(1, TILES, 2)]
            back = [pltpu.roll(now[t], 127, 1) for t in range(0, TILES, 2)]
            back += [pltpu.roll(from_right, 127 - x, 1)]
            around = []
            for t in range(0, TILES, 2):
                around.append(now[t + 1] + jnp.where(is_first, forth[t // 2], forth[t // 2 + 1]))
                around.append(now[t] + jnp.where(is_last, back[t // 2 + 1], back[t // 2]))
            made = []
            for t in range(TILES):
                cut = pl.ds(t * 128, 128)
                beside = (below[t] + above[t]) + around[t]
                beside = beside + (field[base + 1, x + 1, :, cut] + field[base - 1, x + 1, :, cut])
                hopped = onsite[p, x, :, cut] * now[t] - beside
                if n == 0:
                    value = hopped * (1.0 / spectral_scale)
                else:
                    value = hopped * (2.0 / spectral_scale) - older[base, x + 1, :, cut]
                if n + 1 < STEPS:
                    newer[base, x + 1, :, cut] = value
                made.append(value)
            if n + 1 < STEPS:
                left_edge = jnp.where(lane == x, pltpu.roll(made[0], x, 1), left_edge)
                right_edge = jnp.where(lane == x, pltpu.roll(made[TILES - 1], x + 1, 1), right_edge)
            pair.append(made)
            if len(pair) == 2:
                at = (x - 1) * PROBES
                for t in range(TILES):
                    cut = pl.ds(t * 128, 128)
                    high, low = split(jnp.concatenate([pair[0][t], pair[1][t]], 0))
                    halves[p, fresh + at : fresh + at + 16, cut] = high
                    halves[p, fresh + PART + at : fresh + PART + at + 16, cut] = low
                pair = []
            above, now = now, below

        if n + 1 < STEPS:
            send_edges(n + 1, p, left_edge, right_edge)
            if DEFER == 0:
                send_rows(n + 1, p)
            else:
                pl.when(p >= DEFER)(lambda: send_rows(n + 1, p - DEFER))
        if DEFER:
            pl.when(p < DEFER)(lambda: send_rows(n, p + PL - DEFER))

        if n + 1 == STEPS:
            both = moved(halves[p, fresh : fresh + HALF], unmix)
            last[p] = (both[0:PART] + both[PART:HALF]).reshape(ROWS, PROBES, COLS)

        lane_group = lanes() // PROBES
        stays = halves[p, kept : kept + (PART if n == 0 else HALF)]
        own, other = halves[p, kept : kept + PART], halves[p, fresh : fresh + HALF]
        if n % 2 == 0:
            streamed = [(own, (0,)), (other, (0, 1))]
        else:
            streamed = [(halves[p, 0 : HALF + PART], (0, 1, 2))]
        blocks = []
        for left_rows, parts in streamed:
            product = lax.dot_general(left_rows, stays, (((1,), (1,)), ((), ())), preferred_element_type=F32)
            blocks += [product[q * PART : (q + 1) * PART] for q in parts]
        if n % 2:
            blocks = [blocks[2], blocks[0], blocks[1]]

        def equal_rows(block, c):
            chosen = block[0:PROBES, c : c + 128]
            for x in range(1, ROWS):
                chosen = jnp.where(lane_group == x, block[x * PROBES : (x + 1) * PROBES, c : c + 128], chosen)
            return chosen

        grams[n, 0] += equal_rows(blocks[0], 0)
        crossed = equal_rows(blocks[1], 0) + equal_rows(blocks[2], 0)
        if n:
            grams[n, 1] += equal_rows(blocks[0], PART)
            crossed = crossed + equal_rows(blocks[1], PART) + equal_rows(blocks[2], PART)
        grams[n, 2] += crossed

    sub = lax.broadcasted_iota(jnp.int32, (8, 128), 0)
    keep = sub == lanes() // PROBES

    def over_rows(total):
        for shift in (8, 16, 32, 64):
            total = total + pltpu.roll(total, shift, 1)
        return total

    def turned(total):
        return jnp.transpose(jnp.concatenate([total] * ROWS, 0))[0:PROBES]

    packed = jnp.zeros((8, 128), F32)
    for n in range(STEPS):
        pl.loop(0, PL)(functools.partial(step, n))
        even, odd = over_rows(grams[n, 0]), turned(over_rows(grams[n, 2]))
        if n:
            low = over_rows(grams[n, 1])
            even = even + low + turned(low)
        for m, total in ((2 * n, even), (2 * n + 1, odd)):
            row = jnp.sum(jnp.where(keep, total, 0.0), axis=0, keepdims=True)
            packed = jnp.where(sub == m, jnp.broadcast_to(row, (8, 128)), packed)
    flat[...] = packed

    first[gy] = packed
    copies = []
    for d in range(1, GYN):
        c = pltpu.make_async_remote_copy(
            flat, first.at[gy], sum_send.at[0, d], sum_recv.at[0, d],
            device_id=(gx, lax.rem(gy + d, GYN)), device_id_type=MESH,
        )
        c.start()
        copies.append(c)
    for d in range(1, GYN):
        pltpu.make_async_remote_copy(
            flat, first.at[lax.rem(gy + GYN - d, GYN)], sum_send.at[0, d], sum_recv.at[0, d],
            device_id=(gx, lax.rem(gy + d, GYN)), device_id_type=MESH,
        ).wait_recv()
    total = first[0]
    for d in range(1, GYN):
        total = total + first[d]
    second[gx] = total
    for d in range(1, GXN):
        c = pltpu.make_async_remote_copy(
            second.at[gx], second.at[gx], sum_send.at[1, d], sum_recv.at[1, d],
            device_id=(lax.rem(gx + d, GXN), gy), device_id_type=MESH,
        )
        c.start()
        copies.append(c)
    for d in range(1, GXN):
        source = lax.rem(gx + GXN - d, GXN)
        pltpu.make_async_remote_copy(
            second.at[source], second.at[source], sum_send.at[1, d], sum_recv.at[1, d],
            device_id=(lax.rem(gx + d, GXN), gy), device_id_type=MESH,
        ).wait_recv()
    total = second[0]
    for d in range(1, GXN):
        total = total + second[d]
    moments_out[...] = total

    for c in copies:
        c.wait_send()
    for n in range(STEPS):

        @pl.loop(0, PL)
        def _(p):
            for side in range(2):
                row_copy(n, p, side).wait_send()
                col_copy(n, p, side).wait_send()


def finish_kernel(vector, grams, table, green, out, table_here, out_sem, table_sem):
    device = lax.axis_index("gx") * GYN + lax.axis_index("gy")
    fetch = pltpu.make_async_copy(table.at[device], table_here, table_sem)
    fetch.start()
    copies = []
    for p in range(PL):
        for i in range(PROBES):
            c = pltpu.make_async_copy(vector.at[p, :, i, :], out.at[i, p], out_sem.at[p, i])
            c.start()
            copies.append(c)
    fetch.wait()
    scaled = grams[...] / SITES
    rows = [scaled[0:1], scaled[1:2]]
    for m in range(2, NMOM):
        rows.append(2.0 * scaled[m : m + 1] - rows[m % 2])
    moments = jnp.concatenate(rows + [jnp.zeros((128 - NMOM, 128), F32)], 0)
    weights = jnp.transpose(jnp.concatenate([table_here[...], jnp.zeros((128 - NMOM, 128), F32)], 0))
    result = jnp.dot(weights, moments, precision=lax.Precision.HIGHEST, preferred_element_type=F32)
    green[0] = result[0:EB, 0 : PROBES * PROBES]
    green[1] = result[EB : 2 * EB, 0 : PROBES * PROBES]
    for c in copies:
        c.wait()


def on_device(levels, probe_bits):
    anywhere = pl.BlockSpec(memory_space=pl.ANY)
    vmem = pl.BlockSpec(memory_space=pltpu.VMEM)
    dma = pltpu.SemaphoreType.DMA
    last, grams = pl.pallas_call(
        main_kernel,
        out_shape=(
            pltpu.VMEM((PL, ROWS, PROBES, COLS), F32),
            pltpu.VMEM((8, 128), F32),
        ),
        in_specs=[anywhere, anywhere],
        out_specs=(vmem, vmem),
        scratch_shapes=[
            pltpu.VMEM((PL + 2, ROWS + 2, PROBES, COLS), F32),
            pltpu.VMEM((PL + 2, ROWS + 2, PROBES, COLS), F32),
            pltpu.VMEM((PL + 2, ROWS + 2, PROBES, COLS), F32),
            pltpu.VMEM((PL + 2, ROWS + 2, PROBES, COLS), F32),
            pltpu.VMEM((PL, ROWS, PROBES, COLS), jnp.int32),
            pltpu.VMEM((PL, 2 * HALF, COLS), BF16),
            pltpu.VMEM((PL, ROWS, PROBES, COLS), F32),
            pltpu.VMEM((PL, ROWS, COLS), jnp.int32),
            pltpu.VMEM((BLOCK, BLOCK), BF16),
            pltpu.VMEM((BLOCK, BLOCK), BF16),
            pltpu.VMEM((STEPS, 2, PL, 8, 128), F32),
            pltpu.VMEM((STEPS, 2, PL, 8, 128), F32),
            pltpu.VMEM((STEPS, 3, 8, 128), F32),
            pltpu.VMEM((8, 128), F32),
            pltpu.VMEM((GYN, 8, 128), F32),
            pltpu.VMEM((GXN, 8, 128), F32),
            dma((STEPS, 2, PL)),
            dma((STEPS, 2, PL)),
            dma((STEPS, 2, PL)),
            dma((STEPS, 2, PL)),
            dma((PL, PROBES)),
            dma,
            dma((2, GYN)),
            dma((2, GYN)),
        ],
        compiler_params=pltpu.CompilerParams(
            collective_id=0, has_side_effects=True, vmem_limit_bytes=54 << 20
        ),
    )(levels, probe_bits)
    green, out = pl.pallas_call(
        finish_kernel,
        out_shape=(
            jax.ShapeDtypeStruct((2, EB, PROBES * PROBES), F32),
            jax.ShapeDtypeStruct((PROBES, PL, ROWS, COLS), F32),
        ),
        in_specs=[vmem, vmem, anywhere],
        out_specs=(vmem, anywhere),
        scratch_shapes=[
            pltpu.VMEM((NMOM, 2 * EB), F32),
            dma((PL, PROBES)),
            dma,
        ],
        compiler_params=pltpu.CompilerParams(vmem_limit_bytes=8 << 20),
    )(last, grams, jnp.asarray(energy_tables()))
    return green, out


def solution(mesh):
    return jax.shard_map(
        on_device,
        mesh=mesh,
        in_specs=(P(None, "gx", "gy"), P(None, None, "gx", "gy")),
        out_specs=(P(None, ("gx", "gy"), None), P(None, None, "gx", "gy")),
        check_vma=False,
    )
```

time: 69.2 us -> 58.5 us (0.85)
  Pallas kernels: 68.4 us -> 57.8 us
    pallas_call x1, Pallas kernels: 65.3 us -> 54.6 us  [on_device(): pl.pallas_call(main_kernel, out_shape=(pltpu.VMEM((PL, ROWS, PROBES, COLS...]
where the time goes in v2:
time: 58.5 us; the launch traced here: 58.4 us
  Pallas kernels  57.8 us (99%)
  between operations  0.65 us (1%)
    pallas_call x1, Pallas kernels, on_device(): pl.pallas_call(main_kernel, out_shape=(pltpu.VMEM((PL, ROWS, PROBES, COLS...  54.6 us
    pallas_call x1, Pallas kernels, on_device(): pl.pallas_call(finish_kernel, out_shape=(jax.ShapeDtypeStruct((2, EB, PRO...  3.19 us

profile of v2, /device:TPU:1, one launch (start us, length us, event | category | flops | bytes accessed | tf_op | source)
XLA Modules:
  0.0 58.4 jit_solution(5018322768344471395)
XLA Ops:
  0.6 0.0 copy-start
  0.6 54.6 %shard_map.50 = (f32[8,16,8,1024]{3,2,1,0:T(8,128)S(1)}, f32[8,128]{1,0:T(8,128)S(1)}) custom-call(s32[8,16,1024]{2,1,0:T(8,128)} %levels.1, s32[8,8,16,1024]{3,2,1,0:T(8,128)} %bits.1), custom_call_target="tpu_custom_call" | custom-call | tf_op jit(solution)/shard_map/pallas_call | solution.py:380
  55.2 0.0 copy-done
  55.2 3.2 %shard_map.51 = (f32[2,64,64]{2,1,0:T(8,128)}, f32[8,8,16,1024]{3,2,1,0:T(8,128)}) custom-call(f32[8,16,8,1024]{3,2,1,0:T(8,128)S(1)} %get-tuple-element.4.vector, f32[8,128]{1,0:T(8,128)S(1)} %get-tuple-element.5.grams, f32[128,8,128]{2,1,0:T(8,128)S(1)} %copy-done), custom_call_target="tpu_custom_call" | custom-call | tf_op jit(solution)/shard_map/pallas_call | solution.py:418
Async XLA Ops:
  0.6 54.6 %copy-start = (f32[128,8,128]{2,1,0:T(8,128)S(1)}, f32[128,8,128]{2,1,0:T(8,128)}, u32[]{:S(2)}) copy-start(f32[128,8,128]{2,1,0:T(8,128)} %constant.2.clone.table) | copy-start | bytes 1572868

commit v3 on v2

--- a/solution.py
+++ b/solution.py
@@ -115,13 +115,13 @@
     for d in range(1, GYN):
         pl.semaphore_signal(barrier, inc=1, device_id=(gx, lax.rem(gy + d, GYN)), device_id_type=MESH)
 
+    lev_copy = pltpu.make_async_copy(levels, lev, lev_sem)
+    lev_copy.start()
+
     @pl.loop(0, PL)
     def _(p):
         for i in range(PROBES):
             load(p, i).start()
-
-    lev_copy = pltpu.make_async_copy(levels, lev, lev_sem)
-    lev_copy.start()
 
     source = lax.broadcasted_iota(jnp.int32, (BLOCK, BLOCK), 0)
     place = lax.broadcasted_iota(jnp.int32, (BLOCK, BLOCK), 1)
@@ -155,17 +155,6 @@
             right_edge = jnp.where(lane == x, pltpu.roll(row[:, COLS - 128 :], x + 1, 1), right_edge)
         return left_edge, right_edge
 
-    pl.semaphore_wait(barrier, GXN + GYN - 2)
-
-    @pl.loop(0, PL)
-    def _(p):
-        left_edge, right_edge = begin(p)
-        send_edges(0, p, left_edge, right_edge)
-        if DEFER == 0:
-            send_rows(0, p)
-        else:
-            pl.when(p < PL - DEFER)(lambda: send_rows(0, p))
-
     for field in fields:
         for p in (0, PL + 1):
 
@@ -183,6 +172,17 @@
             at = p * ROWS + x
             value = disorder_width * (level[at : at + 1] / (LEVELS - 1) - 0.5) + slope
             onsite[p, x] = jnp.broadcast_to(value, (PROBES, COLS))
+
+    pl.semaphore_wait(barrier, GXN + GYN - 2)
+
+    @pl.loop(0, PL // 2)
+    def _(q):
+        send_edges(0, 2 * q, *begin(2 * q))
+        send_rows(0, q)
+        send_edges(0, 2 * q + 1, *begin(2 * q + 1))
+
+    for p in range(PL // 2, PL - DEFER):
+        send_rows(0, p)
 
     def step(n, p):
         field, base = fields[n], p + 1

time: 58.5 us -> 57.9 us (0.990)
  Pallas kernels: 57.8 us -> 57.1 us
    pallas_call x1, Pallas kernels: 54.6 us -> 53.9 us  [on_device(): pl.pallas_call(main_kernel, out_shape=(pltpu.VMEM((PL, ROWS, PROBES, COLS...]
where the time goes in v3:
time: 57.9 us; the launch traced here: 57.7 us
  Pallas kernels  57.1 us (99%)
  between operations  0.65 us (1%)
    pallas_call x1, Pallas kernels, on_device(): pl.pallas_call(main_kernel, out_shape=(pltpu.VMEM((PL, ROWS, PROBES, COLS...  53.9 us
    pallas_call x1, Pallas kernels, on_device(): pl.pallas_call(finish_kernel, out_shape=(jax.ShapeDtypeStruct((2, EB, PRO...  3.19 us

profile of v3, /device:TPU:1, one launch (start us, length us, event | category | flops | bytes accessed | tf_op | source)
XLA Modules:
  0.0 57.7 jit_solution(3717828510844574959)
XLA Ops:
  0.6 0.0 copy-start
  0.6 53.9 %shard_map.50 = (f32[8,16,8,1024]{3,2,1,0:T(8,128)S(1)}, f32[8,128]{1,0:T(8,128)S(1)}) custom-call(s32[8,16,1024]{2,1,0:T(8,128)} %levels.1, s32[8,8,16,1024]{3,2,1,0:T(8,128)} %bits.1), custom_call_target="tpu_custom_call" | custom-call | tf_op jit(solution)/shard_map/pallas_call | solution.py:380
  54.5 0.0 copy-done
  54.6 3.2 %shard_map.51 = (f32[2,64,64]{2,1,0:T(8,128)}, f32[8,8,16,1024]{3,2,1,0:T(8,128)}) custom-call(f32[8,16,8,1024]{3,2,1,0:T(8,128)S(1)} %get-tuple-element.4.vector, f32[8,128]{1,0:T(8,128)S(1)} %get-tuple-element.5.grams, f32[128,8,128]{2,1,0:T(8,128)S(1)} %copy-done), custom_call_target="tpu_custom_call" | custom-call | tf_op jit(solution)/shard_map/pallas_call | solution.py:418
Async XLA Ops:
  0.6 53.9 %copy-start = (f32[128,8,128]{2,1,0:T(8,128)S(1)}, f32[128,8,128]{2,1,0:T(8,128)}, u32[]{:S(2)}) copy-start(f32[128,8,128]{2,1,0:T(8,128)} %constant.2.clone.table) | copy-start | bytes 1572868

commit v4 on v3

--- a/solution.py
+++ b/solution.py
@@ -311,6 +311,13 @@
         )
         c.start()
         copies.append(c)
+    for n in range(STEPS):
+
+        @pl.loop(0, PL)
+        def _(p):
+            for side in range(2):
+                row_copy(n, p, side).wait_send()
+                col_copy(n, p, side).wait_send()
     for d in range(1, GYN):
         pltpu.make_async_remote_copy(
             flat, first.at[lax.rem(gy + GYN - d, GYN)], sum_send.at[0, d], sum_recv.at[0, d],
@@ -327,6 +334,8 @@
         )
         c.start()
         copies.append(c)
+    for c in copies[: GYN - 1]:
+        c.wait_send()
     for d in range(1, GXN):
         source = lax.rem(gx + GXN - d, GXN)
         pltpu.make_async_remote_copy(
@@ -338,15 +347,8 @@
         total = total + second[d]
     moments_out[...] = total
 
-    for c in copies:
+    for c in copies[GYN - 1 :]:
         c.wait_send()
-    for n in range(STEPS):
-
-        @pl.loop(0, PL)
-        def _(p):
-            for side in range(2):
-                row_copy(n, p, side).wait_send()
-                col_copy(n, p, side).wait_send()
 
 
 def finish_kernel(vector, grams, table, green, out, table_here, out_sem, table_sem):

time: 57.9 us -> 57.5 us (level)
  no operation moved by 1% of the time
where the time goes in v4:
time: 57.5 us; the launch traced here: 57.4 us
  Pallas kernels  56.7 us (99%)
  between operations  0.65 us (1%)
    pallas_call x1, Pallas kernels, on_device(): pl.pallas_call(main_kernel, out_shape=(pltpu.VMEM((PL, ROWS, PROBES, COLS...  53.6 us
    pallas_call x1, Pallas kernels, on_device(): pl.pallas_call(finish_kernel, out_shape=(jax.ShapeDtypeStruct((2, EB, PRO...  3.19 us

profile of v4, /device:TPU:1, one launch (start us, length us, event | category | flops | bytes accessed | tf_op | source)
XLA Modules:
  0.0 57.4 jit_solution(12041644419534145805)
XLA Ops:
  0.6 0.0 copy-start
  0.6 53.6 %shard_map.50 = (f32[8,16,8,1024]{3,2,1,0:T(8,128)S(1)}, f32[8,128]{1,0:T(8,128)S(1)}) custom-call(s32[8,16,1024]{2,1,0:T(8,128)} %levels.1, s32[8,8,16,1024]{3,2,1,0:T(8,128)} %bits.1), custom_call_target="tpu_custom_call" | custom-call | tf_op jit(solution)/shard_map/pallas_call | solution.py:382
  54.2 0.0 copy-done
  54.2 3.2 %shard_map.51 = (f32[2,64,64]{2,1,0:T(8,128)}, f32[8,8,16,1024]{3,2,1,0:T(8,128)}) custom-call(f32[8,16,8,1024]{3,2,1,0:T(8,128)S(1)} %get-tuple-element.4.vector, f32[8,128]{1,0:T(8,128)S(1)} %get-tuple-element.5.grams, f32[128,8,128]{2,1,0:T(8,128)S(1)} %copy-done), custom_call_target="tpu_custom_call" | custom-call | tf_op jit(solution)/shard_map/pallas_call | solution.py:420
Async XLA Ops:
  0.6 53.6 %copy-start = (f32[128,8,128]{2,1,0:T(8,128)S(1)}, f32[128,8,128]{2,1,0:T(8,128)}, u32[]{:S(2)}) copy-start(f32[128,8,128]{2,1,0:T(8,128)} %constant.2.clone.table) | copy-start | bytes 1572868

commit v5 on v4

--- a/solution.py
+++ b/solution.py
@@ -27,7 +27,8 @@
 DEFER = 3
 PART = ROWS * PROBES
 HALF = 2 * PART
-BLOCK = 256
+EACH = 4
+BLOCK = 128 * EACH
 
 disorder_width = 4.0
 field_strength = 3.0
@@ -125,8 +126,8 @@
 
     source = lax.broadcasted_iota(jnp.int32, (BLOCK, BLOCK), 0)
     place = lax.broadcasted_iota(jnp.int32, (BLOCK, BLOCK), 1)
-    mix[...] = jnp.where(source == lax.rem(place, 128) * 2 + place // 128, 1.0, 0.0).astype(BF16)
-    unmix[...] = jnp.where(place == lax.rem(source, 128) * 2 + source // 128, 1.0, 0.0).astype(BF16)
+    mix[...] = jnp.where(source == lax.rem(place, 128) * EACH + place // 128, 1.0, 0.0).astype(BF16)
+    unmix[...] = jnp.where(place == lax.rem(source, 128) * EACH + source // 128, 1.0, 0.0).astype(BF16)
 
     def moved(value, matrix):
         order = matrix[...]
@@ -205,13 +206,15 @@
         for x in range(ROWS):
             below = tiles(x + 2)
             forth = [pltpu.roll(from_left, (128 - x) % 128, 1)]
-            forth += [pltpu.roll(now[t], 1, 1) for t in range(1, TILES, 2)]
-            back = [pltpu.roll(now[t], 127, 1) for t in range(0, TILES, 2)]
+            forth += [pltpu.roll(now[t], 1, 1) for t in range(EACH - 1, TILES, EACH)]
+            back = [pltpu.roll(now[t], 127, 1) for t in range(0, TILES, EACH)]
             back += [pltpu.roll(from_right, 127 - x, 1)]
             around = []
-            for t in range(0, TILES, 2):
-                around.append(now[t + 1] + jnp.where(is_first, forth[t // 2], forth[t // 2 + 1]))
-                around.append(now[t] + jnp.where(is_last, back[t // 2 + 1], back[t // 2]))
+            for t in range(TILES):
+                block = t // EACH
+                before = now[t - 1] if t % EACH else jnp.where(is_first, forth[block], forth[block + 1])
+                beyond = now[t + 1] if (t + 1) % EACH else jnp.where(is_last, back[block + 1], back[block])
+                around.append(beyond + before)
             made = []
             for t in range(TILES):
                 cut = pl.ds(t * 128, 128)

time: 57.5 us -> 57.8 us (level)
  no operation moved by 1% of the time
where the time goes in v5:
time: 57.8 us; the launch traced here: 57.7 us
  Pallas kernels  57 us (99%)
  between operations  0.65 us (1%)
    pallas_call x1, Pallas kernels, on_device(): pl.pallas_call(main_kernel, out_shape=(pltpu.VMEM((PL, ROWS, PROBES, COLS...  53.8 us
    pallas_call x1, Pallas kernels, on_device(): pl.pallas_call(finish_kernel, out_shape=(jax.ShapeDtypeStruct((2, EB, PRO...  3.19 us

profile of v5, /device:TPU:1, one launch (start us, length us, event | category | flops | bytes accessed | tf_op | source)
XLA Modules:
  0.0 57.7 jit_solution(6612323127394091017)
XLA Ops:
  0.6 0.0 copy-start
  0.6 53.8 %shard_map.50 = (f32[8,16,8,1024]{3,2,1,0:T(8,128)S(1)}, f32[8,128]{1,0:T(8,128)S(1)}) custom-call(s32[8,16,1024]{2,1,0:T(8,128)} %levels.1, s32[8,8,16,1024]{3,2,1,0:T(8,128)} %bits.1), custom_call_target="tpu_custom_call" | custom-call | tf_op jit(solution)/shard_map/pallas_call | solution.py:385
  54.5 0.0 copy-done
  54.5 3.2 %shard_map.51 = (f32[2,64,64]{2,1,0:T(8,128)}, f32[8,8,16,1024]{3,2,1,0:T(8,128)}) custom-call(f32[8,16,8,1024]{3,2,1,0:T(8,128)S(1)} %get-tuple-element.4.vector, f32[8,128]{1,0:T(8,128)S(1)} %get-tuple-element.5.grams, f32[128,8,128]{2,1,0:T(8,128)S(1)} %copy-done), custom_call_target="tpu_custom_call" | custom-call | tf_op jit(solution)/shard_map/pallas_call | solution.py:423
Async XLA Ops:
  0.6 53.8 %copy-start = (f32[128,8,128]{2,1,0:T(8,128)S(1)}, f32[128,8,128]{2,1,0:T(8,128)}, u32[]{:S(2)}) copy-start(f32[128,8,128]{2,1,0:T(8,128)} %constant.2.clone.table) | copy-start | bytes 1572868
